TPU v7x, 32 devices: a whole 2x2x4 slice. The times are simulated.
32 devices in a mesh: groups: 2 (over y), brick: 4 (over z), segment: 2 (over x), chan: 2 (over core).
Axes of the slice: x: 2, y: 2, z: 4, core: 2. Of those that a mesh axis runs over, the one named last changes fastest.
Arguments:
- saved_inputs: bfloat16 [2, 1, 96, 1024], P('segment', None, 'chan', ('groups', 'brick')), parts along dimension 3, may hold values from -6 to 6
- cotangent: bfloat16 [1, 96, 1024], P(None, 'chan', ('groups', 'brick')), parts along dimension 2, may hold values from -6 to 6
- weights: bfloat16 [2, 27, 9216], P('segment', None, 'chan'), may hold values from -0.0625 to 0.0625
- neighbors: int32 [1, 27, 1024], P(None, None, ('groups', 'brick')), parts along dimension 2, may hold values from 0 to 160, as said below
- send_lists: int32 [1, 8, 4, 8], P(None, ('groups', 'brick')), parts along dimension 1, may hold values from 0 to 127
Outputs:
- input_grads: bfloat16 [2, 1, 96, 1024], P('segment', None, 'chan', ('groups', 'brick')), parts along dimension 3
- weight_grads: float32 [4, 27, 9216], P(('groups', 'segment'), None, 'chan'), parts along dimension 0
There are 2 independent parts, one for each index of `groups`. A program takes and returns all parts, laid end to end along the dimension named above; an argument that names none is the same for every part. Nothing has to cross between parts.
Inputs may be any that keep to these rules, and one draw needn't show every extreme that they name: `neighbors`: the code at offset 27 // 2 is the voxel's own local row. Codes reach the no-neighbour value in every draw.
All inputs are finite; a program needn't handle non-finite values.
Results may differ from a plain program's by a relative error of at most 0.0095.
Values may be sent and summed in bfloat16 or wider, within the bound.
A program may use at most 64 MiB of HBM per device.

v0:
```python
import jax
import jax.numpy as jnp
from jax import lax
from jax.sharding import PartitionSpec as P


def shifted(block, axis, distance):
    devices = range(lax.axis_size(axis))
    route = [(i - distance, i) for i in devices if i - distance in devices]
    return lax.ppermute(block, axis, route)


def scatter_back(contrib, tap_hot, send_hot, owners, slot_count):
    width = contrib.shape[0]
    row_count = send_hot.shape[1]
    high = lax.Precision.HIGHEST
    contrib_buf = jnp.einsum(
        "ikr,ker->ie", contrib, tap_hot, precision=high, preferred_element_type=jnp.float32
    )
    halo_terms = contrib_buf[:, row_count : row_count + owners * slot_count].reshape(
        width, owners, slot_count
    )
    returned = lax.all_to_all(halo_terms, "brick", split_axis=1, concat_axis=1, tiled=True)
    returned_flat = returned.reshape(width, owners * slot_count)
    placed = jnp.einsum(
        "ip,pr->ir", returned_flat, send_hot, precision=high, preferred_element_type=jnp.float32
    )
    return contrib_buf[:, :row_count] + placed


def shards(saved_inputs, cotangent, weights, neighbors, send_lists):
    segments = lax.axis_size("segment")
    segment_id = lax.axis_index("segment")
    micro_count = saved_inputs.shape[1]
    half_width = saved_inputs.shape[2]
    row_count = saved_inputs.shape[3]
    owners = send_lists.shape[2]
    slot_count = send_lists.shape[3]
    tap_count = weights.shape[1]
    full_width = weights.shape[2] // half_width
    ext_count = row_count + owners * slot_count + 1
    kernel = weights[0].reshape(tap_count, half_width, full_width)
    saved_layer = saved_inputs[0]
    send_all = send_lists[:, 0]
    ext_iota = jnp.arange(ext_count, dtype=jnp.int32)
    row_iota = jnp.arange(row_count, dtype=jnp.int32)

    def tick(tick_id, state_tuple):
        previous, out_buffer, kernel_acc = state_tuple
        micro_raw = tick_id - (segments - 1 - segment_id)
        is_valid = jnp.logical_and(micro_raw >= 0, micro_raw < micro_count)
        micro_id = jnp.clip(micro_raw, 0, micro_count - 1)
        arrived = shifted(previous, "segment", -1)
        top_grad = lax.dynamic_index_in_dim(cotangent, micro_id, 0, keepdims=False)
        upstream = jnp.where(segment_id == segments - 1, top_grad, arrived)
        x_half = lax.dynamic_index_in_dim(saved_layer, micro_id, 0, keepdims=False)
        send_rows = lax.dynamic_index_in_dim(send_all, micro_id, 0, keepdims=False)
        codes = lax.dynamic_index_in_dim(neighbors, micro_id, 0, keepdims=False)
        send_flat = send_rows.reshape(owners * slot_count)
        send_match = send_flat[:, None] == row_iota[None, :]
        send_bf = send_match.astype(jnp.bfloat16)
        send_wide = send_match.astype(jnp.float32)
        tap_match = codes[:, None, :] == ext_iota[None, :, None]
        tap_bf = tap_match.astype(jnp.bfloat16)
        tap_wide = tap_match.astype(jnp.float32)
        x_full = lax.all_gather(x_half, "chan", axis=0, tiled=True)
        picked = jnp.einsum(
            "ir,pr->ip", x_full, send_bf, preferred_element_type=jnp.float32
        ).astype(jnp.bfloat16)
        halo_rows = lax.all_to_all(
            picked.reshape(full_width, owners, slot_count),
            "brick",
            split_axis=1,
            concat_axis=1,
            tiled=True,
        )
        extended = jnp.concatenate(
            [
                x_full,
                halo_rows.reshape(full_width, owners * slot_count),
                jnp.zeros((full_width, 1), jnp.bfloat16),
            ],
            axis=1,
        )
        tap_rows = jnp.einsum(
            "ie,ker->ikr", extended, tap_bf, preferred_element_type=jnp.float32
        ).astype(jnp.bfloat16)
        pre_act = jnp.einsum("ikr,koi->or", tap_rows, kernel, preferred_element_type=jnp.float32)
        sigmoid_val = jax.nn.sigmoid(pre_act)
        up_wide = upstream.astype(jnp.float32)
        grad_pre = (up_wide * sigmoid_val * (1.0 + pre_act * (1.0 - sigmoid_val))).astype(
            jnp.bfloat16
        )
        kernel_new = jnp.einsum(
            "ikr,or->koi", tap_rows, grad_pre, preferred_element_type=jnp.float32
        )
        contrib = jnp.einsum("koi,or->ikr", kernel, grad_pre, preferred_element_type=jnp.float32)
        partial_sum = scatter_back(contrib, tap_wide, send_wide, owners, slot_count)
        conv_grad = lax.psum_scatter(partial_sum, "chan", scatter_dimension=0, tiled=True)
        result = (up_wide + conv_grad).astype(jnp.bfloat16)
        updated = lax.dynamic_update_index_in_dim(out_buffer, result, micro_id, 0)
        out_buffer = jnp.where(is_valid, updated, out_buffer)
        kernel_acc = kernel_acc + jnp.where(is_valid, kernel_new, jnp.zeros_like(kernel_new))
        return (result, out_buffer, kernel_acc)

    start_state = (
        jnp.zeros((half_width, row_count), jnp.bfloat16),
        jnp.zeros((micro_count, half_width, row_count), jnp.bfloat16),
        jnp.zeros(kernel.shape, jnp.float32),
    )
    final_state = lax.fori_loop(0, micro_count + segments - 1, tick, start_state)
    kernel_total = lax.psum(final_state[2], "brick")
    return (final_state[1][None], kernel_total.reshape(tap_count, half_width * full_width)[None])


def solution(mesh):
    return jax.shard_map(
        shards,
        mesh=mesh,
        in_specs=(
            P("segment", None, "chan", ("groups", "brick")),
            P(None, "chan", ("groups", "brick")),
            P("segment", None, "chan"),
            P(None, None, ("groups", "brick")),
            P(None, ("groups", "brick"), None, None),
        ),
        out_specs=(
            P("segment", None, "chan", ("groups", "brick")),
            P(("groups", "segment"), None, "chan"),
        ),
        check_vma=False,
    )
```

profile of v0, /device:TPU:0, one launch (start us, length us, event | category | flops | bytes accessed | tf_op | source)
XLA Modules:
  0.0 132.5 jit_solution(6480555780902265192)
XLA Ops:
  8.0 0.8 eq.136
  8.8 0.7 copy.12
  9.5 1.3 reshape_squeeze.3
  10.8 69.7 %while.21 = (s32[]{:T(128)}, bf16[48,128]{1,0:T(8,128)(2,1)S(1)}, bf16[1,48,128]{2,1,0:T(8,128)(2,1)S(1)}, f32[27,48,96]{2,1,0:T(8,128)S(1)}, pred[]{:T(512)}, /...) while((s32[]{:T(128)}, bf16[48,128]{1,0:T(8,128)(2,1)S(1)}, ...), condition=%wide.wide.region_2.3_spmd.clone, body=%wide.wide.region_0.2_spmd.clone.sunk | while | flops 850924352 | bytes 7266946 | solution.py:111
  10.8 2.2 %all-gather.4 = bf16[1,96,128]{2,1,0:T(8,128)(2,1)S(1)} all-gather(bf16[1,48,128]{2,1,0:T(8,128)(2,1)} %get-tuple-element.532), channel_id=2, replica_groups=mesh['groups'=2,'brick'=4,'segment'=2,'chan'=2] {'chan'}, dimensions={1}, use_global_device_ids=true | all-gather | bytes 36864 | tf_op jit(solution)/shard_map/while/body/eval_jaxpr/all_gather | solution.py:66
  13.0 0.8 fusion.71
  13.8 6.2 %all-to-all-start = ((bf16[96,4,8]{0,2,1:T(8,128)(2,1)}), bf16[96,4,8]{0,2,1:T(8,128)(2,1)S(1)}, u32[]{:S(2)}, u32[]{:S(2)}) async-start(bf16[96,4,8]{0,2,1:T(8,128)(2,1)} %fusion.71), calls=%async_computation | async-start | bytes 16384 | tf_op jit(solution)/shard_map/while/body/eval_jaxpr/all_to_all | solution.py:70
  20.0 1.3 collective-permute-start
  21.3 0.1 copy.18
  21.4 0.1 pad.2.clone.3
  21.4 4.1 %all-to-all-done = bf16[96,4,8]{0,2,1:T(8,128)(2,1)S(1)} async-done(((bf16[96,4,8]{0,2,1:T(8,128)(2,1)}), bf16[96,4,8]{0,2,1:T(8,128)(2,1)S(1)}, u32[]{:S(2)}, u32[]{:S(2)}) %all-to-all-start) | async-done | bytes 6176 | tf_op jit(solution)/shard_map/while/body/eval_jaxpr/all_to_all | solution.py:70
  25.5 0.7 fusion.72
  26.2 0.0 collective-permute-done
  26.2 1.0 fusion.73
  27.3 0.4 convolution_bitcast_fusion.4
  27.6 1.4 %fusion.74 = f32[96,161]{0,1:T(8,128)S(1)} fusion(f32[96,27,128]{2,0,1:T(8,128)S(1)} %convolution_bitcast_fusion.4, s32[27,128]{1,0:T(8,128)S(1)} %bitcast.128), kind=kOutput, calls=%fused_computation.12.clone.clone.1 | convolution fusion | flops 641547648 | bytes 1402752 | tf_op jit(solution)/shard_map/while/body/eval_jaxpr/ikr,ker->ie/dot_general | solution.py:17
  29.0 0.0 copy-start
  29.0 0.6 slice_bitcast_fusion.3
  29.6 4.4 %all-to-all-start.1 = ((f32[96,4,8]{0,2,1:T(8,128)}), f32[96,4,8]{0,2,1:T(8,128)S(1)}, u32[]{:S(2)}, u32[]{:S(2)}) async-start(f32[96,4,8]{0,2,1:T(8,128)} %slice_bitcast_fusion.3), calls=%async_computation.1 | async-start | bytes 32768 | tf_op jit(solution)/shard_map/while/body/eval_jaxpr/all_to_all | solution.py:23
  34.0 0.0 reduce-scatter.2.cloned.1.call-start
  34.1 0.1 copy.19
  34.1 5.5 %all-to-all-done.1 = f32[96,4,8]{0,2,1:T(8,128)S(1)} async-done(((f32[96,4,8]{0,2,1:T(8,128)}), f32[96,4,8]{0,2,1:T(8,128)S(1)}, u32[]{:S(2)}, u32[]{:S(2)}) %all-to-all-start.1) | async-done | bytes 12320 | tf_op jit(solution)/shard_map/while/body/eval_jaxpr/all_to_all | solution.py:23
  39.7 0.9 convolution_add_fusion.3
  40.5 0.0 reduce-scatter.2.cloned.1.call-update
  40.6 0.6 fusion.75
  41.2 4.5 %reduce-scatter.2.cloned.1.call-done = f32[48,128]{1,0:T(8,128)} async-done(((f32[96,128]{1,0:T(8,128)}), f32[48,128]{1,0:T(8,128)}) %reduce-scatter.2.cloned.1.call-update) | async-done | bytes 24592 | tf_op jit(solution)/shard_map/while/body/eval_jaxpr/reduce_scatter | solution.py:99
  45.6 0.0 copy-done
  45.6 0.8 bitcast_select_fusion.4
  46.4 2.0 %all-gather.4 = bf16[1,96,128]{2,1,0:T(8,128)(2,1)S(1)} all-gather(bf16[1,48,128]{2,1,0:T(8,128)(2,1)} %get-tuple-element.532), channel_id=2, replica_groups=mesh['groups'=2,'brick'=4,'segment'=2,'chan'=2] {'chan'}, dimensions={1}, use_global_device_ids=true | all-gather | bytes 36864 | tf_op jit(solution)/shard_map/while/body/eval_jaxpr/all_gather | solution.py:66
  48.4 0.8 fusion.71
  49.2 4.8 %all-to-all-start = ((bf16[96,4,8]{0,2,1:T(8,128)(2,1)}), bf16[96,4,8]{0,2,1:T(8,128)(2,1)S(1)}, u32[]{:S(2)}, u32[]{:S(2)}) async-start(bf16[96,4,8]{0,2,1:T(8,128)(2,1)} %fusion.71), calls=%async_computation | async-start | bytes 16384 | tf_op jit(solution)/shard_map/while/body/eval_jaxpr/all_to_all | solution.py:70
  54.1 1.3 collective-permute-start
  55.4 0.1 copy.18
  55.5 0.1 pad.2.clone.3
  55.6 4.1 %all-to-all-done = bf16[96,4,8]{0,2,1:T(8,128)(2,1)S(1)} async-done(((bf16[96,4,8]{0,2,1:T(8,128)(2,1)}), bf16[96,4,8]{0,2,1:T(8,128)(2,1)S(1)}, u32[]{:S(2)}, u32[]{:S(2)}) %all-to-all-start) | async-done | bytes 6176 | tf_op jit(solution)/shard_map/while/body/eval_jaxpr/all_to_all | solution.py:70
  59.7 0.7 fusion.72
  60.3 0.0 collective-permute-done
  60.3 1.0 fusion.73
  61.4 0.4 convolution_bitcast_fusion.4
  61.8 1.4 %fusion.74 = f32[96,161]{0,1:T(8,128)S(1)} fusion(f32[96,27,128]{2,0,1:T(8,128)S(1)} %convolution_bitcast_fusion.4, s32[27,128]{1,0:T(8,128)S(1)} %bitcast.128), kind=kOutput, calls=%fused_computation.12.clone.clone.1 | convolution fusion | flops 641547648 | bytes 1402752 | tf_op jit(solution)/shard_map/while/body/eval_jaxpr/ikr,ker->ie/dot_general | solution.py:17
  63.1 0.0 copy-start
  63.2 0.6 slice_bitcast_fusion.3
  63.8 4.4 %all-to-all-start.1 = ((f32[96,4,8]{0,2,1:T(8,128)}), f32[96,4,8]{0,2,1:T(8,128)S(1)}, u32[]{:S(2)}, u32[]{:S(2)}) async-start(f32[96,4,8]{0,2,1:T(8,128)} %slice_bitcast_fusion.3), calls=%async_computation.1 | async-start | bytes 32768 | tf_op jit(solution)/shard_map/while/body/eval_jaxpr/all_to_all | solution.py:23
  68.2 0.0 reduce-scatter.2.cloned.1.call-start
  68.2 0.1 copy.19
  68.3 5.5 %all-to-all-done.1 = f32[96,4,8]{0,2,1:T(8,128)S(1)} async-done(((f32[96,4,8]{0,2,1:T(8,128)}), f32[96,4,8]{0,2,1:T(8,128)S(1)}, u32[]{:S(2)}, u32[]{:S(2)}) %all-to-all-start.1) | async-done | bytes 12320 | tf_op jit(solution)/shard_map/while/body/eval_jaxpr/all_to_all | solution.py:23
  73.8 0.9 convolution_add_fusion.3
  74.7 0.0 reduce-scatter.2.cloned.1.call-update
  74.7 0.6 fusion.75
  75.3 4.5 %reduce-scatter.2.cloned.1.call-done = f32[48,128]{1,0:T(8,128)} async-done(((f32[96,128]{1,0:T(8,128)}), f32[48,128]{1,0:T(8,128)}) %reduce-scatter.2.cloned.1.call-update) | async-done | bytes 24592 | tf_op jit(solution)/shard_map/while/body/eval_jaxpr/reduce_scatter | solution.py:99
  79.8 0.0 copy-done
  79.8 0.8 bitcast_select_fusion.4
  80.5 0.0 copy-start.1
  80.5 0.0 all-reduce.2.cloned.1.call-start
  80.6 1.5 %broadcast_in_dim_reshape.3 = f32[1,27,4608]{2,0,1:T(1,128)} reshape(f32[27,48,96]{2,1,0:T(8,128)S(1)} %get-tuple-element.284) | data formatting | bytes 995328 | tf_op jit(solution)/shard_map/broadcast_in_dim;reshape | solution.py:113
  82.1 0.0 all-reduce.2.cloned.1.call-update
  82.1 41.1 %all-reduce.2.cloned.1.call-done = f32[1,27,4608]{2,0,1:T(1,128)} async-done(((f32[1,27,4608]{2,0,1:T(1,128)}), f32[1,27,4608]{2,0,1:T(1,128)}) %all-reduce.2.cloned.1.call-update) | async-done | bytes 497680 | tf_op jit(solution)/shard_map/psum | solution.py:112
  123.2 1.8 %copy.33 = f32[1,27,4608]{2,0,1:T(1,128)} copy(f32[1,27,4608]{2,0,1:T(1,128)} %all-reduce.2.cloned.1.call-done) | data formatting | bytes 995328
  125.1 0.0 copy-done.1
  (7 shorter events, 0.0 us)
Async XLA Ops:
  13.8 11.8 %all-to-all-start = ((bf16[96,4,8]{0,2,1:T(8,128)(2,1)}), bf16[96,4,8]{0,2,1:T(8,128)(2,1)S(1)}, u32[]{:S(2)}, u32[]{:S(2)}) async-start(bf16[96,4,8]{0,2,1:T(8,128)(2,1)} %fusion.71), calls=%async_computation | async-start | bytes 16384 | tf_op jit(solution)/shard_map/while/body/eval_jaxpr/all_to_all | solution.py:70
  20.0 6.3 %collective-permute-start = (bf16[48,128]{1,0:T(8,128)(2,1)S(1)}, bf16[48,128]{1,0:T(8,128)(2,1)S(1)}, u32[]{:S(2)}, u32[]{:S(2)}) collective-permute-start(bf16[48,128]{1,0:T(8,128)(2,1)S(1)} %broadcast_select_fusion.3), channel_id=1, source_target_pairs={{2,0},{3,1},{6,4},{7,5},{10,8},{11,9},{14,12},{15,13},{18,16},{19,... | collective-permute-start | bytes 36872 | tf_op jit(solution)/shard_map/while/body/eval_jaxpr/ppermute | solution.py:10
  29.0 16.6 %copy-start = (bf16[1,48,128]{2,1,0:T(8,128)(2,1)S(1)}, bf16[1,48,128]{2,1,0:T(8,128)(2,1)}, u32[]{:S(2)}) copy-start(bf16[1,48,128]{2,1,0:T(8,128)(2,1)} %get-tuple-element.531) | copy-start | bytes 36868 | tf_op jit(solution)/shard_map/while
  29.6 10.0 %all-to-all-start.1 = ((f32[96,4,8]{0,2,1:T(8,128)}), f32[96,4,8]{0,2,1:T(8,128)S(1)}, u32[]{:S(2)}, u32[]{:S(2)}) async-start(f32[96,4,8]{0,2,1:T(8,128)} %slice_bitcast_fusion.3), calls=%async_computation.1 | async-start | bytes 32768 | tf_op jit(solution)/shard_map/while/body/eval_jaxpr/all_to_all | solution.py:23
  34.0 11.6 %reduce-scatter.2.cloned.1.call-start = ((), (), s32[]{:S(2)}) async-start(), calls=%async_computation.4 | async-start | bytes 73728 | tf_op jit(solution)/shard_map/while/body/eval_jaxpr/reduce_scatter | solution.py:99
  49.2 10.4 %all-to-all-start = ((bf16[96,4,8]{0,2,1:T(8,128)(2,1)}), bf16[96,4,8]{0,2,1:T(8,128)(2,1)S(1)}, u32[]{:S(2)}, u32[]{:S(2)}) async-start(bf16[96,4,8]{0,2,1:T(8,128)(2,1)} %fusion.71), calls=%async_computation | async-start | bytes 16384 | tf_op jit(solution)/shard_map/while/body/eval_jaxpr/all_to_all | solution.py:70
  54.1 6.3 %collective-permute-start = (bf16[48,128]{1,0:T(8,128)(2,1)S(1)}, bf16[48,128]{1,0:T(8,128)(2,1)S(1)}, u32[]{:S(2)}, u32[]{:S(2)}) collective-permute-start(bf16[48,128]{1,0:T(8,128)(2,1)S(1)} %broadcast_select_fusion.3), channel_id=1, source_target_pairs={{2,0},{3,1},{6,4},{7,5},{10,8},{11,9},{14,12},{15,13},{18,16},{19,... | collective-permute-start | bytes 36872 | tf_op jit(solution)/shard_map/while/body/eval_jaxpr/ppermute | solution.py:10
  63.1 16.6 %copy-start = (bf16[1,48,128]{2,1,0:T(8,128)(2,1)S(1)}, bf16[1,48,128]{2,1,0:T(8,128)(2,1)}, u32[]{:S(2)}) copy-start(bf16[1,48,128]{2,1,0:T(8,128)(2,1)} %get-tuple-element.531) | copy-start | bytes 36868 | tf_op jit(solution)/shard_map/while
  63.8 10.0 %all-to-all-start.1 = ((f32[96,4,8]{0,2,1:T(8,128)}), f32[96,4,8]{0,2,1:T(8,128)S(1)}, u32[]{:S(2)}, u32[]{:S(2)}) async-start(f32[96,4,8]{0,2,1:T(8,128)} %slice_bitcast_fusion.3), calls=%async_computation.1 | async-start | bytes 32768 | tf_op jit(solution)/shard_map/while/body/eval_jaxpr/all_to_all | solution.py:23
  68.2 11.6 %reduce-scatter.2.cloned.1.call-start = ((), (), s32[]{:S(2)}) async-start(), calls=%async_computation.4 | async-start | bytes 73728 | tf_op jit(solution)/shard_map/while/body/eval_jaxpr/reduce_scatter | solution.py:99
  80.5 44.5 %copy-start.1 = (bf16[1,48,128]{2,1,0:T(8,128)(2,1)}, bf16[1,48,128]{2,1,0:T(8,128)(2,1)S(1)}, u32[]{:S(2)}) copy-start(bf16[1,48,128]{2,1,0:T(8,128)(2,1)S(1)} %get-tuple-element.283) | copy-start | bytes 36868
  80.5 42.7 %all-reduce.2.cloned.1.call-start = ((), (), s32[]{:S(2)}) async-start(), calls=%async_computation.3 | async-start | bytes 995328 | tf_op jit(solution)/shard_map/psum | solution.py:112
Sparse Core Ops, SparseCore 0:
  40.7 4.9 reduce-scatter.1
  74.8 4.9 reduce-scatter.1
Sparse Core Ops, SparseCore 1:
  83.9 39.2 all-reduce.1
where the time goes:
time: 133 us
  waiting for transfers between devices  69.3 us (52%)
  starting transfers between devices  22.5 us (17%)
  between operations  15.5 us (12%)
  matrix products  11.4 us (9%)
  local copies, waits for them, and re-layouts  7.87 us (6%)
  blocking collectives  4.19 us (3%)
  other arithmetic  1.53 us (1%)
    psum x1, waiting for transfers between devices, shards(): kernel_total = lax.psum(final_state[2], 'brick')  41.1 us
    all_to_all x2, starting transfers between devices, tick(): lax.all_to_all(picked.reshape(full_width, owners, slot_count), 'brick', s...  11 us
    all_to_all x2, waiting for transfers between devices, scatter_back(): lax.all_to_all(halo_terms, 'brick', split_axis=1, concat_axis=1, tiled=True)  11 us
    reduce_scatter x2, waiting for transfers between devices, tick(): lax.psum_scatter(partial_sum, 'chan', scatter_dimension=0, tiled=True)  8.92 us
    all_to_all x2, starting transfers between devices, scatter_back(): lax.all_to_all(halo_terms, 'brick', split_axis=1, concat_axis=1, tiled=True)  8.81 us
    all_to_all x2, waiting for transfers between devices, tick(): lax.all_to_all(picked.reshape(full_width, owners, slot_count), 'brick', s...  8.2 us
    all_gather x2, blocking collectives, tick(): x_full = lax.all_gather(x_half, 'chan', axis=0, tiled=True)  4.19 us
    dot_general x2, matrix products, scatter_back(): jnp.einsum('ikr,ker->ie', contrib, tap_hot, precision=high, preferred_ele...  2.74 us
  transfers between devices with their start and end apart: 9, of which 7 were waited for; matrix products, arithmetic and copies ran while one was open for 2% of the time, Pallas kernels for 0%

commit v1 on v0

v1 whole, which is shorter than its diff:
```python
import functools
import math

import jax
import jax.numpy as jnp
from jax import lax
from jax.experimental import pallas as pl
from jax.experimental.pallas import tpu as pltpu
from jax.sharding import PartitionSpec as P

MESH = pl.DeviceIdType.MESH
F32 = jnp.float32
BF16 = jnp.bfloat16


def round_up(value, unit):
    return -(-value // unit) * unit


def dot(a, b, dims=((1,), (0,))):
    return lax.dot_general(a, b, (dims, ((), ())), preferred_element_type=F32)


def body(
    sizes,
    x_ref, cot_ref, w_ref, code_ref, list_ref,
    out_ref, dw_ref,
    xs, meta, w_rows, w_flat, w_turn, hot, taps, factor, up_buf, g_in, g_out, gp, gs,
    halo_out, halo_in, part_out, part_in, half_own,
    x_send, x_recv, m_send, m_recv, p_send, p_recv, h_send, h_recv,
    l_send, l_recv, s_send, s_recv,
):
    owners, chans, segments, half, full, rows, slots, tap_count = sizes
    peers = owners * chans
    ext = rows + owners * slots
    code_rows = round_up(tap_count, 8)
    stride = round_up(tap_count, 8)
    me = lax.axis_index("brick")
    ch = lax.axis_index("chan")
    seg = lax.axis_index("segment")
    top = seg == segments - 1
    mine = me * chans + ch

    def peer(step):
        other = lax.rem(mine + step, peers)
        return other, other // chans, lax.rem(other, chans)

    def brick(step):
        return lax.rem(me + step, owners)

    barrier = pltpu.get_barrier_semaphore()
    for step in range(1, peers):
        _, b, c = peer(step)
        pl.semaphore_signal(barrier, 1, device_id={"brick": b, "chan": c}, device_id_type=MESH)

    @pl.when(seg > 0)
    def _():
        pl.semaphore_signal(barrier, 1, device_id={"segment": seg - 1}, device_id_type=MESH)

    @pl.when(seg < segments - 1)
    def _():
        pl.semaphore_signal(barrier, 1, device_id={"segment": seg + 1}, device_id_type=MESH)

    lanes = lax.broadcasted_iota(jnp.int32, (owners, 128), 1)
    listed = jnp.concatenate([list_ref[0, 0]] * (128 // slots), axis=1)
    is_mine = lanes // slots == me
    meta[me, 0:tap_count, :] = code_ref[0]
    meta[me, code_rows : code_rows + owners, :] = jnp.where(is_mine, listed + me * rows, 0)
    own_list = jnp.where(is_mine, listed, -1)

    neighbours = (
        peers - 1 + jnp.where(seg > 0, 1, 0) + jnp.where(seg < segments - 1, 1, 0)
    )
    pl.semaphore_wait(barrier, neighbours)

    copies = []
    for step in range(1, peers):
        _, b, c = peer(step)
        copies.append(pltpu.make_async_remote_copy(
            src_ref=x_ref.at[0, 0], dst_ref=xs.at[mine],
            send_sem=x_send.at[step], recv_sem=x_recv.at[mine],
            device_id={"brick": b, "chan": c}, device_id_type=MESH))
        copies[-1].start()
    for step in range(1, owners):
        copies.append(pltpu.make_async_remote_copy(
            src_ref=meta.at[me], dst_ref=meta.at[me],
            send_sem=m_send.at[step], recv_sem=m_recv.at[me],
            device_id={"brick": brick(step)}, device_id_type=MESH))
        copies[-1].start()
    xs[mine] = x_ref[0, 0]

    group = math.lcm(full, 128) // full
    for first in range(0, half, group):
        count = min(group, half - first)
        block = w_ref[0, :, first * full : (first + count) * full].astype(F32)
        for j in range(count):
            at = (first + j) * stride
            w_rows[at : at + tap_count, 0:full] = block[:, j * full : (j + 1) * full]
    for k in range(tap_count):
        w_flat[k * half : (k + 1) * half, :] = (
            w_rows[pl.ds(k, half, stride=stride), :].astype(BF16)
        )
    w_turn[...] = jnp.transpose(w_flat[:, 0:full].astype(F32)).astype(BF16)

    ext_iota = lax.broadcasted_iota(jnp.int32, (ext, rows), 0)

    def one_hot(codes_of, k):
        return jnp.where(codes_of[k : k + 1, :] == ext_iota, 1.0, 0.0).astype(BF16)

    codes = code_ref[0]
    for k in range(tap_count):
        hot[:, k * rows : (k + 1) * rows] = one_hot(codes, k)

    def wait_slot(dst, sem):
        pltpu.make_async_copy(dst, dst, sem).wait()

    for step in range(1, peers):
        other, _, _ = peer(step)
        wait_slot(xs.at[other], x_recv.at[other])
    for step in range(1, owners):
        other = brick(step)
        wait_slot(meta.at[other], m_recv.at[other])

    def features(q):
        return jnp.concatenate([xs[q * chans + c] for c in range(chans)], axis=0)

    def extended(q):
        every = jnp.concatenate([features(o) for o in range(owners)], axis=1)
        row = meta[0, pl.ds(code_rows + q, 1), :]
        for o in range(1, owners):
            row = row + meta[o, pl.ds(code_rows + q, 1), :]
        at = lax.broadcasted_iota(jnp.int32, (owners * rows, 128), 0)
        pick = jnp.where(at == row, 1.0, 0.0).astype(BF16)
        halo = dot(every, pick).astype(BF16)
        return jnp.concatenate([features(q), halo[:, 0 : owners * slots]], axis=1)

    own_ext = extended(me)
    own_taps = dot(own_ext, hot[...]).astype(BF16)
    lane_me = pl.ds(pl.multiple_of(me * rows, rows), rows)
    pre = jnp.zeros((half, rows), F32)
    for k in range(tap_count):
        tap_k = own_taps[:, k * rows : (k + 1) * rows]
        pre = pre + dot(w_flat[k * half : (k + 1) * half, 0:full], tap_k)
        taps[k * full : (k + 1) * full, lane_me] = tap_k
    sig = jax.nn.sigmoid(pre)
    factor[...] = sig * (1.0 + pre * (1.0 - sig))

    def other_taps():
        def one(step, carry):
            q = brick(step)
            ext_q = extended(q)
            codes_q = meta[q]
            lane_q = pl.ds(pl.multiple_of(q * rows, rows), rows)
            for k in range(tap_count):
                taps[k * full : (k + 1) * full, lane_q] = dot(
                    ext_q, one_hot(codes_q, k)
                ).astype(BF16)
            return carry

        lax.fori_loop(1, owners, one, 0)

    down = pltpu.make_async_remote_copy(
        src_ref=g_out, dst_ref=g_in, send_sem=s_send, recv_sem=s_recv,
        device_id={"segment": jnp.maximum(seg - 1, 0)}, device_id_type=MESH)

    @pl.when(top)
    def _():
        up_buf[...] = cot_ref[0]

    @pl.when(jnp.logical_not(top))
    def _():
        other_taps()
        wait_slot(g_in, s_recv)
        up_buf[...] = g_in[...]

    up = up_buf[...].astype(F32)
    grad = (up * factor[...]).astype(BF16)
    gp[me] = grad
    for step in range(1, owners):
        copies.append(pltpu.make_async_remote_copy(
            src_ref=gp.at[me], dst_ref=gp.at[me],
            send_sem=p_send.at[step], recv_sem=p_recv.at[me],
            device_id={"brick": brick(step)}, device_id_type=MESH))
        copies[-1].start()

    for k in range(tap_count):
        gs[k * half : (k + 1) * half, :] = dot(
            grad, hot[:, k * rows : (k + 1) * rows], ((1,), (1,))
        ).astype(BF16)
    terms = dot(w_turn[...], gs[...])
    local, halo = terms[:, 0:rows], terms[:, rows:ext]
    fill = 128 - owners * slots
    if fill:
        halo = jnp.concatenate([halo, jnp.zeros((full, fill), F32)], axis=1)
    halo = halo.astype(BF16)
    for c in range(chans):
        halo_out[c] = halo[c * half : (c + 1) * half]
        part_out[c] = local[c * half : (c + 1) * half]
    for step in range(1, chans):
        c = lax.rem(ch + step, chans)
        copies.append(pltpu.make_async_remote_copy(
            src_ref=part_out.at[c], dst_ref=part_in.at[ch],
            send_sem=l_send.at[step], recv_sem=l_recv.at[ch],
            device_id={"chan": c}, device_id_type=MESH))
        copies[-1].start()
    for step in range(1, peers):
        _, b, c = peer(step)
        copies.append(pltpu.make_async_remote_copy(
            src_ref=halo_out.at[c], dst_ref=halo_in.at[mine],
            send_sem=h_send.at[step], recv_sem=h_recv.at[mine],
            device_id={"brick": b, "chan": c}, device_id_type=MESH))
        copies[-1].start()
    halo_in[mine] = halo_out[ch]
    half_own[...] = part_out[ch] + up

    row_iota = lax.broadcasted_iota(jnp.int32, (rows, 128), 0)

    def finish():
        place = jnp.concatenate(
            [jnp.where(own_list[q : q + 1, :] == row_iota, 1.0, 0.0).astype(BF16)
             for q in range(owners)], axis=1)
        for step in range(1, chans):
            c = lax.rem(ch + step, chans)
            wait_slot(part_in.at[c], l_recv.at[c])
        for step in range(1, peers):
            other, _, _ = peer(step)
            wait_slot(halo_in.at[other], h_recv.at[other])
        total = half_own[...]
        for step in range(1, chans):
            total = total + part_in[lax.rem(ch + step, chans)]
        came = []
        for q in range(owners):
            term = halo_in[q * chans].astype(F32)
            for c in range(1, chans):
                term = term + halo_in[q * chans + c].astype(F32)
            came.append(term.astype(BF16))
        total = total + dot(jnp.concatenate(came, axis=1), place, ((1,), (1,)))
        g_out[...] = total.astype(BF16)

        @pl.when(seg > 0)
        def _():
            down.start()

        out_ref[0, 0] = total.astype(BF16)

    @pl.when(top)
    def _():
        finish()
        other_taps()

    for step in range(1, owners):
        other = brick(step)
        wait_slot(gp.at[other], p_recv.at[other])
    every_grad = jnp.concatenate([gp[q] for q in range(owners)], axis=1)
    for k in range(tap_count):
        w_rows[pl.ds(k, half, stride=stride), 0:full] = dot(
            every_grad, taps[k * full : (k + 1) * full, :], ((1,), (1,))
        )
    for first in range(0, half, group):
        count = min(group, half - first)
        dw_ref[0, :, first * full : (first + count) * full] = jnp.concatenate(
            [w_rows[(first + j) * stride : (first + j) * stride + tap_count, 0:full]
             for j in range(count)], axis=1)

    @pl.when(jnp.logical_not(top))
    def _():
        finish()

    for copy in copies:
        copy.wait_send()

    @pl.when(seg > 0)
    def _():
        down.wait_send()


def shards(sizes, saved_inputs, cotangent, weights, neighbors, send_lists):
    owners, chans, segments, half, full, rows, slots, tap_count = sizes
    peers = owners * chans
    ext = rows + owners * slots
    stride = round_up(tap_count, 8)
    meta_rows = stride + round_up(owners, 8)
    dma = pltpu.SemaphoreType.DMA
    vmem = pl.BlockSpec(memory_space=pltpu.VMEM)
    return pl.pallas_call(
        functools.partial(body, sizes),
        out_shape=(
            jax.ShapeDtypeStruct((1, 1, half, rows), BF16),
            jax.ShapeDtypeStruct((1, tap_count, half * full), F32),
        ),
        in_specs=[vmem] * 5,
        out_specs=(vmem, vmem),
        scratch_shapes=[
            pltpu.VMEM((peers, half, rows), BF16),
            pltpu.VMEM((owners, meta_rows, 128), jnp.int32),
            pltpu.VMEM((half * stride, 128), F32),
            pltpu.VMEM((tap_count * half, 128), BF16),
            pltpu.VMEM((full, tap_count * half), BF16),
            pltpu.VMEM((ext, tap_count * rows), BF16),
            pltpu.VMEM((tap_count * full, owners * rows), BF16),
            pltpu.VMEM((half, rows), F32),
            pltpu.VMEM((half, rows), BF16),
            pltpu.VMEM((half, rows), BF16),
            pltpu.VMEM((half, rows), BF16),
            pltpu.VMEM((owners, half, rows), BF16),
            pltpu.VMEM((tap_count * half, ext), BF16),
            pltpu.VMEM((chans, half, 128), BF16),
            pltpu.VMEM((peers, half, 128), BF16),
            pltpu.VMEM((chans, half, rows), F32),
            pltpu.VMEM((chans, half, rows), F32),
            pltpu.VMEM((half, rows), F32),
            dma((peers,)), dma((peers,)), dma((owners,)), dma((owners,)),
            dma((owners,)), dma((owners,)), dma((peers,)), dma((peers,)),
            dma((chans,)), dma((chans,)), dma, dma,
        ],
        compiler_params=pltpu.CompilerParams(
            collective_id=0, has_side_effects=True, vmem_limit_bytes=48 * 1024 * 1024
        ),
    )(saved_inputs, cotangent, weights, neighbors, send_lists)


def solution(mesh):
    def call(saved_inputs, cotangent, weights, neighbors, send_lists):
        axes = mesh.shape
        half = saved_inputs.shape[2] // axes["chan"]
        owners, slots = send_lists.shape[2], send_lists.shape[3]
        rows = saved_inputs.shape[3] // (axes["groups"] * axes["brick"])
        sizes = (
            owners, axes["chan"], axes["segment"], half, saved_inputs.shape[2], rows, slots,
            weights.shape[1],
        )
        return jax.shard_map(
            functools.partial(shards, sizes),
            mesh=mesh,
            in_specs=(
                P("segment", None, "chan", ("groups", "brick")),
                P(None, "chan", ("groups", "brick")),
                P("segment", None, "chan"),
                P(None, None, ("groups", "brick")),
                P(None, ("groups", "brick"), None, None),
            ),
            out_specs=(
                P("segment", None, "chan", ("groups", "brick")),
                P(("groups", "segment"), None, "chan"),
            ),
            check_vma=False,
        )(saved_inputs, cotangent, weights, neighbors, send_lists)

    return call
```

time: 133 us -> 30 us (0.23)
  waiting for transfers between devices: 69.3 us -> 0 us
  Pallas kernels: 0 us -> 25.4 us
  starting transfers between devices: 22.5 us -> 0 us
  between operations: 15.5 us -> 0.68 us
  matrix products: 11.4 us -> 0 us
  local copies, waits for them, and re-layouts: 7.87 us -> 3.59 us
  blocking collectives: 4.19 us -> 0 us
  other arithmetic: 1.53 us -> 0 us
    psum x1 -> x0, waiting for transfers between devices: 41.1 us -> none  [shards(): kernel_total = lax.psum(final_state[2], 'brick')]
    pallas_call x0 -> x1, Pallas kernels: none -> 25.4 us  [shards(): pl.pallas_call(functools.partial(body, sizes), out_shape=(jax.ShapeDtypeS...]
    all_to_all x4 -> x0, starting transfers between devices: 19.9 us -> none  [the longest x2 11 us: tick(): lax.all_to_all(picked.reshape(full_width, owners, slot_count), 'brick', s...]
    all_to_all x4 -> x0, waiting for transfers between devices: 19.2 us -> none  [the longest x2 11 us: scatter_back(): lax.all_to_all(halo_terms, 'brick', split_axis=1, concat_axis=1, tiled=True)]
    dot_general x14 -> x0, matrix products: 11.4 us -> none  [the longest x2 2.74 us: scatter_back(): jnp.einsum('ikr,ker->ie', contrib, tap_hot, precision=high, preferred_ele...]
    reduce_scatter x2 -> x0, waiting for transfers between devices: 8.92 us -> none  [tick(): lax.psum_scatter(partial_sum, 'chan', scatter_dimension=0, tiled=True)]
    all_gather x2 -> x0, blocking collectives: 4.19 us -> none  [tick(): x_full = lax.all_gather(x_half, 'chan', axis=0, tiled=True)]
    another operation x2 -> x0, local copies, waits for them, and re-layouts: 2.77 us -> none  [the longest x1 1.49 us: shards(): kernel_total.reshape(tap_count, half_width * full_width)[None]]
  transfers between devices with their start and end apart: 9 -> 0, of which waited for: 7 -> 0; matrix products, arithmetic and copies ran while one was open for 2% -> 0% of each run, Pallas kernels for 0% -> 0%
where the time goes in v1:
time: 30 us; the launch traced here: 29.7 us
  Pallas kernels  25.4 us (85%)
  local copies, waits for them, and re-layouts  3.59 us (12%)
  between operations  0.68 us (2%)
    pallas_call x1, Pallas kernels, shards(): pl.pallas_call(functools.partial(body, sizes), out_shape=(jax.ShapeDtypeS...  25.4 us
    unnamed x10, local copies, waits for them, and re-layouts  2.3 us
    pallas_call x1, local copies, waits for them, and re-layouts, shards(): pl.pallas_call(functools.partial(body, sizes), out_shape=(jax.ShapeDtypeS...  1.29 us

profile of v1, /device:TPU:0, one launch (start us, length us, event | category | flops | bytes accessed | tf_op | source)
XLA Modules:
  0.0 29.7 jit_solution(9211427968074889543)
XLA Ops:
  0.6 0.0 copy-start.3
  0.6 0.0 copy-start.2
  0.7 0.0 copy-start.1
  0.7 0.7 %copy.7.code_ref = s32[1,27,128]{2,1,0:T(8,128)S(1)} copy(s32[1,27,128]{2,0,1:T(1,128)} %param.8) | data formatting | bytes 27648 | tf_op args[3]
  1.4 0.0 copy-done.3
  1.4 0.0 copy-done.2
  1.4 0.0 copy-done.1
  1.4 0.0 copy-start
  1.4 1.0 %copy-done = bf16[1,27,4608]{2,1,0:T(8,128)(2,1)S(1)} copy-done((bf16[1,27,4608]{2,1,0:T(8,128)(2,1)S(1)}, bf16[1,27,4608]{2,1,0:T(8,128)(2,1)}, u32[]{:S(2)}) %copy-start) | copy-done | bytes 248856
  2.4 25.4 %shard_map.68 = (bf16[1,1,48,128]{3,2,1,0:T(8,128)(2,1)S(1)}, f32[1,27,4608]{2,1,0:T(8,128)S(1)}) custom-call(bf16[1,1,48,128]{3,2,1,0:T(8,128)(2,1)S(1)} %copy-done.1, bf16[1,48,128]{2,1,0:T(8,128)(2,1)S(1)} %copy-done.2, bf16[1,27,4608]{2,1,0:T(8,128)(2,1)S(1)} %copy-done, s32[1,27,128]{2,1,0:T(8,128)S(1)} %copy.7.code_ref, s32[1,1,4,8]{3,2,1,0:T(4,128)S(1)} %copy-done.3), custom_call_target="tpu_custom_call" | custom-call | tf_op jit(solution)/shard_map/pallas_call | solution.py:285
  27.8 1.3 %copy.8 = f32[1,27,4608]{2,0,1:T(1,128)} copy(f32[1,27,4608]{2,1,0:T(8,128)S(1)} %get-tuple-element.3) | data formatting | bytes 995328 | tf_op jit(solution)/shard_map/pallas_call | solution.py:285
  29.1 0.6 %copy.10 = bf16[1,1,48,128]{3,2,1,0:T(8,128)(2,1)} copy(bf16[1,1,48,128]{3,2,1,0:T(8,128)(2,1)S(1)} %get-tuple-element.6) | data formatting | bytes 24576
Async XLA Ops:
  0.6 0.8 %copy-start.3 = (s32[1,1,4,8]{3,2,1,0:T(4,128)S(1)}, s32[1,1,4,8]{3,2,1,0:T(4,128)}, u32[]{:S(2)}) copy-start(s32[1,1,4,8]{3,2,1,0:T(4,128)} %list_ref.1) | copy-start | bytes 388
  0.6 0.8 %copy-start.2 = (bf16[1,48,128]{2,1,0:T(8,128)(2,1)S(1)}, bf16[1,48,128]{2,1,0:T(8,128)(2,1)}, u32[]{:S(2)}) copy-start(bf16[1,48,128]{2,1,0:T(8,128)(2,1)} %cot_ref.1) | copy-start | bytes 36868
  0.7 0.7 %copy-start.1 = (bf16[1,1,48,128]{3,2,1,0:T(8,128)(2,1)S(1)}, bf16[1,1,48,128]{3,2,1,0:T(8,128)(2,1)}, u32[]{:S(2)}) copy-start(bf16[1,1,48,128]{3,2,1,0:T(8,128)(2,1)} %x_ref.1) | copy-start | bytes 36868
  1.4 1.0 %copy-start = (bf16[1,27,4608]{2,1,0:T(8,128)(2,1)S(1)}, bf16[1,27,4608]{2,1,0:T(8,128)(2,1)}, u32[]{:S(2)}) copy-start(bf16[1,27,4608]{2,1,0:T(8,128)(2,1)} %w_ref.1) | copy-start | bytes 746500

commit v2 on v1

v2 whole, which is shorter than its diff:
```python
import functools
import math

import jax
import jax.numpy as jnp
from jax import lax
from jax.experimental import pallas as pl
from jax.experimental.pallas import tpu as pltpu
from jax.sharding import PartitionSpec as P

MESH = pl.DeviceIdType.MESH
F32 = jnp.float32
BF16 = jnp.bfloat16


def round_up(value, unit):
    return -(-value // unit) * unit


def dot(a, b, dims=((1,), (0,))):
    return lax.dot_general(a, b, (dims, ((), ())), preferred_element_type=F32)


def body(
    sizes,
    x_ref, cot_ref, w_ref, code_ref, list_ref,
    out_ref, dw_ref,
    packs, codes, listed, cot, w_in, w_rows, w_flat, w_turn, hot, taps, factor, up_buf, g_in, g_out,
    gp, g_rows, g_class, dw_rows, gs, pick_out, pick_in, halo_out, halo_in, part_out, part_in, half_own,
    in_sem, k_send, k_recv, x_send, x_recv, f_send, f_recv, p_send, p_recv, h_send, h_recv,
    l_send, l_recv, s_send, s_recv,
):
    owners, chans, segments, half, full, rows, slots, tap_count = sizes
    peers = owners * chans
    listed_count = owners * slots
    ext = rows + listed_count
    share = code_share(tap_count, chans)
    stride = round_up(tap_count, 8)
    me = lax.axis_index("brick")
    ch = lax.axis_index("chan")
    seg = lax.axis_index("segment")
    top = seg == segments - 1
    mine = me * chans + ch

    def peer(step):
        other = lax.rem(mine + step, peers)
        return other, other // chans, lax.rem(other, chans)

    def brick(step):
        return lax.rem(me + step, owners)

    def core(step):
        return lax.rem(ch + step, chans)

    copies = []

    def send(src, dst, out_sem, in_sem, device):
        copies.append(pltpu.make_async_remote_copy(
            src_ref=src, dst_ref=dst, send_sem=out_sem, recv_sem=in_sem,
            device_id=device, device_id_type=MESH))
        copies[-1].start()

    def arrived(dst, sem):
        pltpu.make_async_copy(dst, dst, sem).wait()

    barrier = pltpu.get_barrier_semaphore()
    for step in range(1, peers):
        _, b, c = peer(step)
        pl.semaphore_signal(barrier, 1, device_id={"brick": b, "chan": c}, device_id_type=MESH)

    @pl.when(seg > 0)
    def _():
        pl.semaphore_signal(barrier, 1, device_id={"segment": seg - 1}, device_id_type=MESH)

    @pl.when(seg < segments - 1)
    def _():
        pl.semaphore_signal(barrier, 1, device_id={"segment": seg + 1}, device_id_type=MESH)

    loads = [
        pltpu.make_async_copy(x_ref.at[0, 0], packs.at[mine, pl.ds(0, half)], in_sem.at[0]),
        pltpu.make_async_copy(code_ref, codes.at[pl.ds(0, tap_count)], in_sem.at[1]),
        pltpu.make_async_copy(w_ref.at[0], w_in, in_sem.at[2]),
        pltpu.make_async_copy(cot_ref.at[0], cot, in_sem.at[3]),
        pltpu.make_async_copy(list_ref.at[0, 0], listed, in_sem.at[4]),
    ]
    for load in loads:
        load.start()
    loads[4].wait()

    lanes = lax.broadcasted_iota(jnp.int32, (owners, 128), 1)
    receiver = lax.broadcasted_iota(jnp.int32, (owners, 128), 0)
    spread = jnp.concatenate([listed[...]] * (128 // slots), axis=1)
    flat = jnp.sum(jnp.where(lanes // slots == receiver, spread, 0), axis=0, keepdims=True)
    row_iota = lax.broadcasted_iota(jnp.int32, (rows, 128), 0)
    send_hot = jnp.where(flat == row_iota, 1.0, 0.0).astype(BF16)[:, 0:listed_count]
    list_rows = round_up(owners, 16)
    held = jnp.where(lanes // slots == me, spread, 0).astype(F32)
    if list_rows > owners:
        held = jnp.concatenate([held, jnp.zeros((list_rows - owners, 128), F32)], axis=0)

    for load in loads[0:2]:
        load.wait()
    packs[mine, half + share : half + share + list_rows, :] = held.astype(BF16)
    own_codes = jnp.concatenate(
        [codes[k] for k in range(tap_count)]
        + [jnp.zeros((chans * share - tap_count, 128), jnp.int32)], axis=0)
    part_codes = own_codes[0:share]
    for c in range(1, chans):
        part_codes = jnp.where(ch == c, own_codes[c * share : (c + 1) * share], part_codes)
    packs[mine, half : half + share, :] = part_codes.astype(F32).astype(BF16)
    picked = dot(packs[mine, 0:half, :], send_hot)
    picked = jnp.concatenate([picked, jnp.zeros((half, 128 - listed_count), F32)], axis=1) if (
        listed_count < 128) else picked
    picked = jnp.concatenate([picked, jnp.zeros((128 - half, 128), F32)], axis=0)
    picked = jnp.transpose(picked)
    for q in range(owners):
        pick_out[q] = picked[q * slots : (q + 1) * slots]

    neighbours = (
        peers - 1 + jnp.where(seg > 0, 1, 0) + jnp.where(seg < segments - 1, 1, 0)
    )
    pl.semaphore_wait(barrier, neighbours)

    for step in range(1, peers):
        _, b, c = peer(step)
        send(pick_out.at[b], pick_in.at[mine], k_send.at[step], k_recv.at[mine],
             {"brick": b, "chan": c})
    for step in range(1, chans):
        send(packs.at[mine], packs.at[mine], f_send.at[step], f_recv.at[mine],
             {"chan": core(step)})
    for step in range(1, owners):
        send(packs.at[mine], packs.at[mine], x_send.at[step], x_recv.at[me],
             {"brick": brick(step)})
    pick_in[mine] = pick_out[me]

    loads[2].wait()
    group = math.lcm(full, 128) // full
    for first in range(0, half, group):
        block = w_in[:, first * full : (first + group) * full].astype(F32)
        for j in range(group):
            at = (first + j) * stride
            w_rows[at : at + tap_count, 0:full] = block[:, j * full : (j + 1) * full]
    for k in range(tap_count):
        w_flat[k * half : (k + 1) * half, :] = (
            w_rows[pl.ds(k, half, stride=stride), :].astype(BF16)
        )
    w_turn[...] = jnp.transpose(w_flat[:, 0:full].astype(F32)).astype(BF16)

    ext_iota = lax.broadcasted_iota(jnp.int32, (ext, rows), 0)

    def one_hot(codes_of, k):
        return jnp.where(codes_of[k : k + 1, :] == ext_iota, 1.0, 0.0).astype(BF16)

    for k in range(tap_count):
        hot[:, k * rows : (k + 1) * rows] = one_hot(own_codes, k)

    def features(q):
        return jnp.concatenate([packs[q * chans + c, 0:half, :] for c in range(chans)], axis=0)

    for step in range(1, chans):
        other = me * chans + core(step)
        arrived(packs.at[other], f_recv.at[other])
    for step in range(1, peers):
        other, _, _ = peer(step)
        arrived(pick_in.at[other], k_recv.at[other])
    own_halo = jnp.concatenate(
        [jnp.transpose(jnp.concatenate(
            [pick_in[q * chans + c] for q in range(owners)], axis=0))[0:half]
         for c in range(chans)], axis=0).astype(BF16)
    own_ext = jnp.concatenate([features(me), own_halo], axis=1)
    own_taps = dot(own_ext, hot[...]).astype(BF16)
    lane_me = pl.ds(pl.multiple_of(me * rows, rows), rows)
    pre = jnp.zeros((half, rows), F32)
    for k in range(tap_count):
        tap_k = own_taps[:, k * rows : (k + 1) * rows]
        pre = pre + dot(w_flat[k * half : (k + 1) * half, 0:full], tap_k)
        taps[k * full : (k + 1) * full, lane_me] = tap_k
    sig = jax.nn.sigmoid(pre)
    factor[...] = sig * (1.0 + pre * (1.0 - sig))

    def forwards():
        return [
            pltpu.make_async_remote_copy(
                src_ref=packs.at[brick(step) * chans + ch],
                dst_ref=packs.at[brick(step) * chans + ch],
                send_sem=f_send.at[chans + (step - 1) * (chans - 1) + turn - 1],
                recv_sem=f_recv.at[brick(step) * chans + ch],
                device_id={"chan": core(turn)}, device_id_type=MESH)
            for step in range(1, owners) for turn in range(1, chans)
        ]

    def other_taps():
        passing = forwards()
        for step in range(1, owners):
            arrived(packs.at[brick(step) * chans + ch], x_recv.at[brick(step)])
            for turn in range(1, chans):
                passing[(step - 1) * (chans - 1) + turn - 1].start()
        for step in range(1, owners):
            for turn in range(1, chans):
                other = brick(step) * chans + core(turn)
                arrived(packs.at[other], f_recv.at[other])
        every = jnp.concatenate([features(o) for o in range(owners)], axis=1)
        at = lax.broadcasted_iota(jnp.int32, (owners * rows, 128), 0)
        list_at = half + share
        lists = packs[0, list_at : list_at + list_rows, :].astype(F32)
        for o in range(1, owners):
            lists = lists + packs[o * chans, list_at : list_at + list_rows, :].astype(F32)
        list_of = lax.broadcasted_iota(jnp.int32, (list_rows, 128), 0)
        owner_lane = lax.broadcasted_iota(jnp.int32, (1, 128), 1) // slots * rows

        def one(step, carry):
            q = brick(step)
            row = jnp.sum(jnp.where(list_of == q, lists, 0.0), axis=0, keepdims=True)
            row = row.astype(jnp.int32) + owner_lane
            pick = jnp.where(at == row, 1.0, 0.0).astype(BF16)
            halo = dot(every, pick).astype(BF16)
            ext_q = jnp.concatenate([features(q), halo[:, 0:listed_count]], axis=1)
            codes_q = jnp.concatenate(
                [packs[q * chans + c, half : half + share, :] for c in range(chans)], axis=0
            ).astype(F32).astype(jnp.int32)
            lane_q = pl.ds(pl.multiple_of(q * rows, rows), rows)
            for k in range(tap_count):
                taps[k * full : (k + 1) * full, lane_q] = dot(
                    ext_q, one_hot(codes_q, k)
                ).astype(BF16)
            return carry

        lax.fori_loop(1, owners, one, 0)
        for copy in passing:
            copy.wait_send()

    down = pltpu.make_async_remote_copy(
        src_ref=g_out, dst_ref=g_in, send_sem=s_send, recv_sem=s_recv,
        device_id={"segment": jnp.maximum(seg - 1, 0)}, device_id_type=MESH)

    loads[3].wait()

    @pl.when(top)
    def _():
        up_buf[...] = cot[...]

    @pl.when(jnp.logical_not(top))
    def _():
        other_taps()
        arrived(g_in, s_recv)
        up_buf[...] = g_in[...]

    up = up_buf[...].astype(F32)
    grad = (up * factor[...]).astype(BF16)
    gp[me] = grad
    for step in range(1, owners):
        send(gp.at[me], gp.at[me], p_send.at[step], p_recv.at[me], {"brick": brick(step)})

    for k in range(tap_count):
        gs[k * half : (k + 1) * half, :] = dot(
            grad, hot[:, k * rows : (k + 1) * rows], ((1,), (1,))
        ).astype(BF16)
    terms = dot(w_turn[...], gs[...])
    local, halo = terms[:, 0:rows], terms[:, rows:ext]
    if listed_count < 128:
        halo = jnp.concatenate([halo, jnp.zeros((full, 128 - listed_count), F32)], axis=1)
    halo = jnp.transpose(jnp.concatenate([halo, jnp.zeros((128 - full, 128), F32)], axis=0))
    for q in range(owners):
        halo_out[q] = halo[q * slots : (q + 1) * slots]
    for step in range(1, peers):
        _, b, c = peer(step)
        send(halo_out.at[b], halo_in.at[mine], h_send.at[step], h_recv.at[mine],
             {"brick": b, "chan": c})
    for c in range(chans):
        part_out[c] = local[c * half : (c + 1) * half]
    for step in range(1, chans):
        c = core(step)
        send(part_out.at[c], part_in.at[ch], l_send.at[step], l_recv.at[ch], {"chan": c})
    halo_in[mine] = halo_out[me]
    half_own[...] = part_out[ch] + up

    def finish():
        for step in range(1, chans):
            c = core(step)
            arrived(part_in.at[c], l_recv.at[c])
        for step in range(1, peers):
            other, _, _ = peer(step)
            arrived(halo_in.at[other], h_recv.at[other])
        total = half_own[...]
        for step in range(1, chans):
            total = total + part_in[core(step)]
        came = []
        for q in range(owners):
            term = halo_in[q * chans]
            for c in range(1, chans):
                term = term + halo_in[q * chans + c]
            came.append(term)
        came = jnp.transpose(jnp.concatenate(came, axis=0))
        own = came[0:half]
        for c in range(1, chans):
            own = jnp.where(ch == c, came[c * half : (c + 1) * half], own)
        total = total + dot(own.astype(BF16), send_hot, ((1,), (1,)))
        g_out[...] = total.astype(BF16)

        @pl.when(seg > 0)
        def _():
            down.start()

        out_ref[0, 0] = total.astype(BF16)

    @pl.when(top)
    def _():
        finish()
        other_taps()

    for step in range(1, owners):
        other = brick(step)
        arrived(gp.at[other], p_recv.at[other])
    for q in range(owners):
        for_q = gp[q].astype(F32)
        g_rows[q * half : (q + 1) * half, :] = for_q
    many = half // group
    step_rows = round_up(many, 8)
    for q in range(owners):
        for a in range(group):
            g_class[a * step_rows : a * step_rows + many, q * rows : (q + 1) * rows] = (
                g_rows[pl.ds(q * half + a, many, stride=group), :]
            )
    every_grad = g_class[...].astype(BF16)
    wide = group * full // 128
    for k in range(tap_count):
        block = dot(every_grad, taps[k * full : (k + 1) * full, :], ((1,), (1,)))
        for r in range(wide):
            pieces, at = [], r * 128
            while at < (r + 1) * 128:
                a, lane = at // full, at % full
                end = min((a + 1) * full, (r + 1) * 128)
                pieces.append(block[a * step_rows : (a + 1) * step_rows, lane : lane + end - at])
                at = end
            dw_rows[pl.ds(k * many * wide + r, many, stride=wide), :] = jnp.concatenate(
                pieces, axis=1)[0:many]
    for at in range(tap_count * many * wide // 4):
        dw_ref[at] = dw_rows[at * 4 : at * 4 + 4, :]

    @pl.when(jnp.logical_not(top))
    def _():
        finish()

    for copy in copies:
        copy.wait_send()

    @pl.when(seg > 0)
    def _():
        down.wait_send()


def code_share(tap_count, chans):
    return round_up(-(-tap_count // chans), 16)


def shards(sizes, saved_inputs, cotangent, weights, neighbors, send_lists):
    owners, chans, segments, half, full, rows, slots, tap_count = sizes
    peers = owners * chans
    ext = rows + owners * slots
    stride = round_up(tap_count, 8)
    share = code_share(tap_count, chans)
    group = math.lcm(full, 128) // full
    dma = pltpu.SemaphoreType.DMA
    vmem = pl.BlockSpec(memory_space=pltpu.VMEM)
    free = pl.BlockSpec(memory_space=pltpu.HBM)
    out, dw = pl.pallas_call(
        functools.partial(body, sizes),
        out_shape=(
            jax.ShapeDtypeStruct((1, 1, half, rows), BF16),
            jax.ShapeDtypeStruct((tap_count * half * full // 512, 4, 128), F32),
        ),
        in_specs=[free] * 5,
        out_specs=(vmem, vmem),
        scratch_shapes=[
            pltpu.VMEM((peers, half + share + round_up(owners, 16), 128), BF16),
            pltpu.VMEM((chans * share, 1, 128), jnp.int32),
            pltpu.VMEM((owners, slots), jnp.int32),
            pltpu.VMEM((half, rows), BF16),
            pltpu.VMEM((tap_count, half * full), BF16),
            pltpu.VMEM((half * stride, 128), F32),
            pltpu.VMEM((tap_count * half, 128), BF16),
            pltpu.VMEM((full, tap_count * half), BF16),
            pltpu.VMEM((ext, tap_count * rows), BF16),
            pltpu.VMEM((tap_count * full, owners * rows), BF16),
            pltpu.VMEM((half, rows), F32),
            pltpu.VMEM((half, rows), BF16),
            pltpu.VMEM((half, rows), BF16),
            pltpu.VMEM((half, rows), BF16),
            pltpu.VMEM((owners, half, rows), BF16),
            pltpu.VMEM((owners * half, rows), F32),
            pltpu.VMEM((group * round_up(half // group, 8), owners * rows), F32),
            pltpu.VMEM((tap_count * half * full // 128, 128), F32),
            pltpu.VMEM((tap_count * half, ext), BF16),
            pltpu.VMEM((owners, slots, 128), F32),
            pltpu.VMEM((peers, slots, 128), F32),
            pltpu.VMEM((owners, slots, 128), F32),
            pltpu.VMEM((peers, slots, 128), F32),
            pltpu.VMEM((chans, half, rows), F32),
            pltpu.VMEM((chans, half, rows), F32),
            pltpu.VMEM((half, rows), F32),
            dma((5,)), dma((peers,)), dma((peers,)), dma((owners,)), dma((owners,)),
            dma((chans + owners * chans,)), dma((peers,)),
            dma((owners,)), dma((owners,)), dma((peers,)), dma((peers,)),
            dma((chans,)), dma((chans,)), dma, dma,
        ],
        compiler_params=pltpu.CompilerParams(
            collective_id=0, has_side_effects=True, vmem_limit_bytes=63 * 1024 * 1024
        ),
    )(
        saved_inputs, cotangent, weights,
        jnp.transpose(neighbors, (1, 0, 2)), send_lists,
    )
    return out, dw.reshape(1, tap_count, half * full)


def solution(mesh):
    def call(saved_inputs, cotangent, weights, neighbors, send_lists):
        axes = mesh.shape
        half = saved_inputs.shape[2] // axes["chan"]
        owners, slots = send_lists.shape[2], send_lists.shape[3]
        rows = saved_inputs.shape[3] // (axes["groups"] * axes["brick"])
        sizes = (
            owners, axes["chan"], axes["segment"], half, saved_inputs.shape[2], rows, slots,
            weights.shape[1],
        )
        return jax.shard_map(
            functools.partial(shards, sizes),
            mesh=mesh,
            in_specs=(
                P("segment", None, "chan", ("groups", "brick")),
                P(None, "chan", ("groups", "brick")),
                P("segment", None, "chan"),
                P(None, None, ("groups", "brick")),
                P(None, ("groups", "brick"), None, None),
            ),
            out_specs=(
                P("segment", None, "chan", ("groups", "brick")),
                P(("groups", "segment"), None, "chan"),
            ),
            check_vma=False,
        )(saved_inputs, cotangent, weights, neighbors, send_lists)

    return call
```

time: 30 us -> 27.5 us (0.917)
  Pallas kernels: 25.4 us -> 23.4 us
  local copies, waits for them, and re-layouts: 3.59 us -> 3.16 us
    pallas_call x1, Pallas kernels: 25.4 us -> 23.4 us  [shards(): pl.pallas_call(functools.partial(body, sizes), out_shape=(jax.ShapeDtypeS...]
    pallas_call x1 -> x0, local copies, waits for them, and re-layouts: 1.29 us -> none  [shards(): pl.pallas_call(functools.partial(body, sizes), out_shape=(jax.ShapeDtypeS...]
    unnamed x10 -> x2, local copies, waits for them, and re-layouts: 2.3 us -> 3.16 us
where the time goes in v2:
time: 27.5 us; the launch traced here: 27.2 us
  Pallas kernels  23.4 us (85%)
  local copies, waits for them, and re-layouts  3.16 us (11%)
  between operations  0.64 us (2%)
    pallas_call x1, Pallas kernels, shards(): pl.pallas_call(functools.partial(body, sizes), out_shape=(jax.ShapeDtypeS...  23.4 us
    unnamed x2, local copies, waits for them, and re-layouts  3.16 us

profile of v2, /device:TPU:0, one launch (start us, length us, event | category | flops | bytes accessed | tf_op | source)
XLA Modules:
  0.0 27.2 jit_solution(4188280282223484474)
XLA Ops:
  0.6 23.4 %shard_map.68 = (bf16[1,1,48,128]{3,2,1,0:T(8,128)(2,1)}, f32[243,4,128]{2,1,0:T(4,128)}) custom-call(bf16[1,1,48,128]{3,2,1,0:T(8,128)(2,1)} %x_ref.1, bf16[1,48,128]{2,1,0:T(8,128)(2,1)} %cot_ref.1, bf16[1,27,4608]{2,1,0:T(8,128)(2,1)} %w_ref.1, s32[27,1,128]{2,1,0:T(1,128)} %bitcast.3, s32[1,1,4,8]{3,2,1,0:T(4,128)} %list_ref.1), custom_call_target="tpu_custom_call" | custom-call | tf_op jit(solution)/shard_map/pallas_call | solution.py:366
  24.1 1.3 %copy.11 = bf16[1,1,48,128]{3,2,1,0:T(8,128)(2,1)} copy(bf16[1,1,48,128]{3,2,1,0:T(8,128)(2,1)} %get-tuple-element.12) | data formatting | bytes 24576
  25.4 1.8 %copy.12 = f32[1,27,4608]{2,0,1:T(1,128)} copy(f32[1,27,4608]{2,0,1:T(1,128)} %bitcast.2) | data formatting | bytes 995328

commit v3 on v2

--- a/solution.py
+++ b/solution.py
@@ -25,10 +25,10 @@
     sizes,
     x_ref, cot_ref, w_ref, code_ref, list_ref,
     out_ref, dw_ref,
-    packs, codes, listed, cot, w_in, w_rows, w_flat, w_turn, hot, taps, factor, up_buf, g_in, g_out,
-    gp, g_rows, g_class, dw_rows, gs, pick_out, pick_in, halo_out, halo_in, part_out, part_in, half_own,
+    packs, codes, listed, cot, w_in, w_rows, w_flat, w_turn, hot, taps, factor, up_buf,
+    gp, g_rows, g_class, dw_rows, gs, pick_out, pick_in, halo_out, halo_in, part_out, part_in, half_own, low_halo, low_part,
     in_sem, k_send, k_recv, x_send, x_recv, f_send, f_recv, p_send, p_recv, h_send, h_recv,
-    l_send, l_recv, s_send, s_recv,
+    l_send, l_recv, lh_send, lh_recv, lp_send, lp_recv,
 ):
     owners, chans, segments, half, full, rows, slots, tap_count = sizes
     peers = owners * chans
@@ -68,13 +68,13 @@
         _, b, c = peer(step)
         pl.semaphore_signal(barrier, 1, device_id={"brick": b, "chan": c}, device_id_type=MESH)
 
-    @pl.when(seg > 0)
-    def _():
-        pl.semaphore_signal(barrier, 1, device_id={"segment": seg - 1}, device_id_type=MESH)
-
     @pl.when(seg < segments - 1)
     def _():
-        pl.semaphore_signal(barrier, 1, device_id={"segment": seg + 1}, device_id_type=MESH)
+        for step in range(peers):
+            _, b, c = peer(step)
+            pl.semaphore_signal(
+                barrier, 1, device_id={"segment": seg + 1, "brick": b, "chan": c},
+                device_id_type=MESH)
 
     loads = [
         pltpu.make_async_copy(x_ref.at[0, 0], packs.at[mine, pl.ds(0, half)], in_sem.at[0]),
@@ -116,9 +116,7 @@
     for q in range(owners):
         pick_out[q] = picked[q * slots : (q + 1) * slots]
 
-    neighbours = (
-        peers - 1 + jnp.where(seg > 0, 1, 0) + jnp.where(seg < segments - 1, 1, 0)
-    )
+    neighbours = peers - 1 + jnp.where(seg > 0, peers, 0)
     pl.semaphore_wait(barrier, neighbours)
 
     for step in range(1, peers):
@@ -229,9 +227,33 @@
         for copy in passing:
             copy.wait_send()
 
-    down = pltpu.make_async_remote_copy(
-        src_ref=g_out, dst_ref=g_in, send_sem=s_send, recv_sem=s_recv,
-        device_id={"segment": jnp.maximum(seg - 1, 0)}, device_id_type=MESH)
+    def low(src, dst, out_sem, in_sem, b, c):
+        return pltpu.make_async_remote_copy(
+            src_ref=src, dst_ref=dst, send_sem=out_sem, recv_sem=in_sem,
+            device_id={"segment": jnp.maximum(seg - 1, 0), "brick": b, "chan": c},
+            device_id_type=MESH)
+
+    lows = []
+    for step in range(peers):
+        _, b, c = peer(step)
+        lows.append(low(halo_out.at[b], low_halo.at[mine], lh_send.at[step], lh_recv.at[mine], b, c))
+    lows.append(low(half_own, low_part.at[ch], lp_send.at[0], lp_recv.at[ch], me, ch))
+    for step in range(1, chans):
+        c = core(step)
+        lows.append(low(part_out.at[c], low_part.at[ch], lp_send.at[step], lp_recv.at[ch], me, c))
+
+    def placed(halos):
+        came = []
+        for q in range(owners):
+            term = halos[q * chans]
+            for c in range(1, chans):
+                term = term + halos[q * chans + c]
+            came.append(term)
+        came = jnp.transpose(jnp.concatenate(came, axis=0))
+        own = came[0:half]
+        for c in range(1, chans):
+            own = jnp.where(ch == c, came[c * half : (c + 1) * half], own)
+        return dot(own.astype(BF16), send_hot, ((1,), (1,)))
 
     loads[3].wait()
 
@@ -242,8 +264,14 @@
     @pl.when(jnp.logical_not(top))
     def _():
         other_taps()
-        arrived(g_in, s_recv)
-        up_buf[...] = g_in[...]
+        for c in range(chans):
+            arrived(low_part.at[c], lp_recv.at[c])
+        for other in range(peers):
+            arrived(low_halo.at[other], lh_recv.at[other])
+        above = low_part[0]
+        for c in range(1, chans):
+            above = above + low_part[c]
+        up_buf[...] = (above + placed(low_halo)).astype(BF16)
 
     up = up_buf[...].astype(F32)
     grad = (up * factor[...]).astype(BF16)
@@ -262,50 +290,26 @@
     halo = jnp.transpose(jnp.concatenate([halo, jnp.zeros((128 - full, 128), F32)], axis=0))
     for q in range(owners):
         halo_out[q] = halo[q * slots : (q + 1) * slots]
+    for c in range(chans):
+        part_out[c] = local[c * half : (c + 1) * half]
+    half_own[...] = part_out[ch] + up
+
+    @pl.when(seg > 0)
+    def _():
+        for copy in lows:
+            copy.start()
+
     for step in range(1, peers):
         _, b, c = peer(step)
         send(halo_out.at[b], halo_in.at[mine], h_send.at[step], h_recv.at[mine],
              {"brick": b, "chan": c})
-    for c in range(chans):
-        part_out[c] = local[c * half : (c + 1) * half]
     for step in range(1, chans):
         c = core(step)
         send(part_out.at[c], part_in.at[ch], l_send.at[step], l_recv.at[ch], {"chan": c})
     halo_in[mine] = halo_out[me]
-    half_own[...] = part_out[ch] + up
-
-    def finish():
-        for step in range(1, chans):
-            c = core(step)
-            arrived(part_in.at[c], l_recv.at[c])
-        for step in range(1, peers):
-            other, _, _ = peer(step)
-            arrived(halo_in.at[other], h_recv.at[other])
-        total = half_own[...]
-        for step in range(1, chans):
-            total = total + part_in[core(step)]
-        came = []
-        for q in range(owners):
-            term = halo_in[q * chans]
-            for c in range(1, chans):
-                term = term + halo_in[q * chans + c]
-            came.append(term)
-        came = jnp.transpose(jnp.concatenate(came, axis=0))
-        own = came[0:half]
-        for c in range(1, chans):
-            own = jnp.where(ch == c, came[c * half : (c + 1) * half], own)
-        total = total + dot(own.astype(BF16), send_hot, ((1,), (1,)))
-        g_out[...] = total.astype(BF16)
-
-        @pl.when(seg > 0)
-        def _():
-            down.start()
-
-        out_ref[0, 0] = total.astype(BF16)
 
     @pl.when(top)
     def _():
-        finish()
         other_taps()
 
     for step in range(1, owners):
@@ -337,16 +341,24 @@
     for at in range(tap_count * many * wide // 4):
         dw_ref[at] = dw_rows[at * 4 : at * 4 + 4, :]
 
-    @pl.when(jnp.logical_not(top))
-    def _():
-        finish()
+    for step in range(1, chans):
+        c = core(step)
+        arrived(part_in.at[c], l_recv.at[c])
+    for step in range(1, peers):
+        other, _, _ = peer(step)
+        arrived(halo_in.at[other], h_recv.at[other])
+    total = half_own[...]
+    for step in range(1, chans):
+        total = total + part_in[core(step)]
+    out_ref[0, 0] = (total + placed(halo_in)).astype(BF16)
 
     for copy in copies:
         copy.wait_send()
 
     @pl.when(seg > 0)
     def _():
-        down.wait_send()
+        for copy in lows:
+            copy.wait_send()
 
 
 def code_share(tap_count, chans):
@@ -384,8 +396,6 @@
             pltpu.VMEM((tap_count * full, owners * rows), BF16),
             pltpu.VMEM((half, rows), F32),
             pltpu.VMEM((half, rows), BF16),
-            pltpu.VMEM((half, rows), BF16),
-            pltpu.VMEM((half, rows), BF16),
             pltpu.VMEM((owners, half, rows), BF16),
             pltpu.VMEM((owners * half, rows), F32),
             pltpu.VMEM((group * round_up(half // group, 8), owners * rows), F32),
@@ -398,17 +408,20 @@
             pltpu.VMEM((chans, half, rows), F32),
             pltpu.VMEM((chans, half, rows), F32),
             pltpu.VMEM((half, rows), F32),
+            pltpu.VMEM((peers, slots, 128), F32),
+            pltpu.VMEM((chans, half, rows), F32),
             dma((5,)), dma((peers,)), dma((peers,)), dma((owners,)), dma((owners,)),
             dma((chans + owners * chans,)), dma((peers,)),
             dma((owners,)), dma((owners,)), dma((peers,)), dma((peers,)),
-            dma((chans,)), dma((chans,)), dma, dma,
+            dma((chans,)), dma((chans,)),
+            dma((peers,)), dma((peers,)), dma((chans,)), dma((chans,)),
         ],
         compiler_params=pltpu.CompilerParams(
-            collective_id=0, has_side_effects=True, vmem_limit_bytes=63 * 1024 * 1024
+            collective_id=0, has_side_effects=True, vmem_limit_bytes=48 * 1024 * 1024
         ),
     )(
-        saved_inputs, cotangent, weights,
-        jnp.transpose(neighbors, (1, 0, 2)), send_lists,
+        *[pltpu.with_memory_space_constraint(v, pltpu.HBM) for v in (saved_inputs, cotangent, weights,
+        jnp.transpose(neighbors, (1, 0, 2)), send_lists)]
     )
     return out, dw.reshape(1, tap_count, half * full)
 

time: 27.5 us -> 23.1 us (0.84)
  Pallas kernels: 23.4 us -> 20.9 us
  local copies, waits for them, and re-layouts: 3.16 us -> 1.38 us
    pallas_call x1, Pallas kernels: 23.4 us -> 20.9 us  [shards(): pl.pallas_call(functools.partial(body, sizes), out_shape=(jax.ShapeDtypeS...]
    unnamed x2, local copies, waits for them, and re-layouts: 3.16 us -> 1.38 us
where the time goes in v3:
time: 23.1 us; the launch traced here: 22.9 us
  Pallas kernels  20.9 us (90%)
  local copies, waits for them, and re-layouts  1.38 us (6%)
  between operations  0.64 us (3%)
    pallas_call x1, Pallas kernels, shards(): pl.pallas_call(functools.partial(body, sizes), out_shape=(jax.ShapeDtypeS...  20.9 us
    unnamed x2, local copies, waits for them, and re-layouts  1.38 us

profile of v3, /device:TPU:0, one launch (start us, length us, event | category | flops | bytes accessed | tf_op | source)
XLA Modules:
  0.0 22.9 jit_solution(16589740446865117756)
XLA Ops:
  0.6 20.9 %shard_map.68 = (bf16[1,1,48,128]{3,2,1,0:T(8,128)(2,1)S(1)}, f32[243,4,128]{2,1,0:T(4,128)S(1)}) custom-call(bf16[1,1,48,128]{3,2,1,0:T(8,128)(2,1)} %x_ref.1, bf16[1,48,128]{2,1,0:T(8,128)(2,1)} %cot_ref.1, bf16[1,27,4608]{2,1,0:T(8,128)(2,1)} %w_ref.1, s32[27,1,128]{2,1,0:T(1,128)} %bitcast.3, s32[1,1,4,8]{3,2,1,0:T(4,128)} %list_ref.1), custom_call_target="tpu_custom_call" | custom-call | tf_op jit(solution)/shard_map/pallas_call | solution.py:378
  21.5 0.6 %copy.11 = bf16[1,1,48,128]{3,2,1,0:T(8,128)(2,1)} copy(bf16[1,1,48,128]{3,2,1,0:T(8,128)(2,1)S(1)} %get-tuple-element.12) | data formatting | bytes 24576
  22.2 0.8 %copy.12 = f32[1,27,4608]{2,0,1:T(1,128)} copy(f32[1,27,4608]{2,0,1:T(1,128)S(1)} %bitcast.2) | data formatting | bytes 995328

commit v4 on v3

--- a/solution.py
+++ b/solution.py
@@ -25,7 +25,7 @@
     sizes,
     x_ref, cot_ref, w_ref, code_ref, list_ref,
     out_ref, dw_ref,
-    packs, codes, listed, cot, w_in, w_rows, w_flat, w_turn, hot, taps, factor, up_buf,
+    packs, codes, listed, cot, w_in, w_rows, w_flat, w_turn, hot, hot_turn, taps, factor, up_buf,
     gp, g_rows, g_class, dw_rows, gs, pick_out, pick_in, halo_out, halo_in, part_out, part_in, half_own, low_halo, low_part,
     in_sem, k_send, k_recv, x_send, x_recv, f_send, f_recv, p_send, p_recv, h_send, h_recv,
     l_send, l_recv, lh_send, lh_recv, lp_send, lp_recv,
@@ -151,6 +151,13 @@
 
     for k in range(tap_count):
         hot[:, k * rows : (k + 1) * rows] = one_hot(own_codes, k)
+    turned = jnp.concatenate(
+        [own_codes, jnp.full((128 - chans * share, 128), -1, jnp.int32)], axis=0)
+    turned = jnp.transpose(turned.astype(F32)).astype(jnp.int32)
+    lane_iota = lax.broadcasted_iota(jnp.int32, (rows, ext), 1)
+    for k in range(tap_count):
+        hot_turn[k * rows : (k + 1) * rows, :] = jnp.where(
+            turned[:, k : k + 1] == lane_iota, 1.0, 0.0).astype(BF16)
 
     def features(q):
         return jnp.concatenate([packs[q * chans + c, 0:half, :] for c in range(chans)], axis=0)
@@ -281,7 +288,7 @@
 
     for k in range(tap_count):
         gs[k * half : (k + 1) * half, :] = dot(
-            grad, hot[:, k * rows : (k + 1) * rows], ((1,), (1,))
+            grad, hot_turn[k * rows : (k + 1) * rows, :]
         ).astype(BF16)
     terms = dot(w_turn[...], gs[...])
     local, halo = terms[:, 0:rows], terms[:, rows:ext]
@@ -393,6 +400,7 @@
             pltpu.VMEM((tap_count * half, 128), BF16),
             pltpu.VMEM((full, tap_count * half), BF16),
             pltpu.VMEM((ext, tap_count * rows), BF16),
+            pltpu.VMEM((tap_count * rows, ext), BF16),
             pltpu.VMEM((tap_count * full, owners * rows), BF16),
             pltpu.VMEM((half, rows), F32),
             pltpu.VMEM((half, rows), BF16),

time: 23.1 us -> 22.6 us (0.978)
  Pallas kernels: 20.9 us -> 20.5 us
    pallas_call x1, Pallas kernels: 20.9 us -> 20.5 us  [shards(): pl.pallas_call(functools.partial(body, sizes), out_shape=(jax.ShapeDtypeS...]
where the time goes in v4:
time: 22.6 us; the launch traced here: 22.5 us
  Pallas kernels  20.5 us (91%)
  local copies, waits for them, and re-layouts  1.38 us (6%)
  between operations  0.64 us (3%)
    pallas_call x1, Pallas kernels, shards(): pl.pallas_call(functools.partial(body, sizes), out_shape=(jax.ShapeDtypeS...  20.5 us
    unnamed x2, local copies, waits for them, and re-layouts  1.38 us

profile of v4, /device:TPU:0, one launch (start us, length us, event | category | flops | bytes accessed | tf_op | source)
XLA Modules:
  0.0 22.5 jit_solution(743033566568829961)
XLA Ops:
  0.6 20.5 %shard_map.68 = (bf16[1,1,48,128]{3,2,1,0:T(8,128)(2,1)S(1)}, f32[243,4,128]{2,1,0:T(4,128)S(1)}) custom-call(bf16[1,1,48,128]{3,2,1,0:T(8,128)(2,1)} %x_ref.1, bf16[1,48,128]{2,1,0:T(8,128)(2,1)} %cot_ref.1, bf16[1,27,4608]{2,1,0:T(8,128)(2,1)} %w_ref.1, s32[27,1,128]{2,1,0:T(1,128)} %bitcast.3, s32[1,1,4,8]{3,2,1,0:T(4,128)} %list_ref.1), custom_call_target="tpu_custom_call" | custom-call | tf_op jit(solution)/shard_map/pallas_call | solution.py:385
  21.1 0.6 %copy.11 = bf16[1,1,48,128]{3,2,1,0:T(8,128)(2,1)} copy(bf16[1,1,48,128]{3,2,1,0:T(8,128)(2,1)S(1)} %get-tuple-element.12) | data formatting | bytes 24576
  21.7 0.8 %copy.12 = f32[1,27,4608]{2,0,1:T(1,128)} copy(f32[1,27,4608]{2,0,1:T(1,128)S(1)} %bitcast.2) | data formatting | bytes 995328

commit v5 on v4

--- a/solution.py
+++ b/solution.py
@@ -126,9 +126,20 @@
     for step in range(1, chans):
         send(packs.at[mine], packs.at[mine], f_send.at[step], f_recv.at[mine],
              {"chan": core(step)})
-    for step in range(1, owners):
-        send(packs.at[mine], packs.at[mine], x_send.at[step], x_recv.at[me],
-             {"brick": brick(step)})
+    shared = [
+        pltpu.make_async_remote_copy(
+            src_ref=packs.at[mine], dst_ref=packs.at[mine],
+            send_sem=x_send.at[step], recv_sem=x_recv.at[me],
+            device_id={"brick": brick(step)}, device_id_type=MESH)
+        for step in range(1, owners)
+    ]
+    copies.extend(shared)
+
+    @pl.when(jnp.logical_not(top))
+    def _():
+        for copy in shared:
+            copy.start()
+
     pick_in[mine] = pick_out[me]
 
     loads[2].wait()
@@ -168,6 +179,12 @@
     for step in range(1, peers):
         other, _, _ = peer(step)
         arrived(pick_in.at[other], k_recv.at[other])
+
+    @pl.when(top)
+    def _():
+        for copy in shared:
+            copy.start()
+
     own_halo = jnp.concatenate(
         [jnp.transpose(jnp.concatenate(
             [pick_in[q * chans + c] for q in range(owners)], axis=0))[0:half]

time: 22.6 us -> 23.6 us (1.044)
  Pallas kernels: 20.5 us -> 21.5 us
    pallas_call x1, Pallas kernels: 20.5 us -> 21.5 us  [shards(): pl.pallas_call(functools.partial(body, sizes), out_shape=(jax.ShapeDtypeS...]
where the time goes in v5:
time: 23.6 us; the launch traced here: 23.5 us
  Pallas kernels  21.5 us (91%)
  local copies, waits for them, and re-layouts  1.38 us (6%)
  between operations  0.64 us (3%)
    pallas_call x1, Pallas kernels, shards(): pl.pallas_call(functools.partial(body, sizes), out_shape=(jax.ShapeDtypeS...  21.5 us
    unnamed x2, local copies, waits for them, and re-layouts  1.38 us

profile of v5, /device:TPU:0, one launch (start us, length us, event | category | flops | bytes accessed | tf_op | source)
XLA Modules:
  0.0 23.5 jit_solution(10453569962165424611)
XLA Ops:
  0.6 21.5 %shard_map.68 = (bf16[1,1,48,128]{3,2,1,0:T(8,128)(2,1)S(1)}, f32[243,4,128]{2,1,0:T(4,128)S(1)}) custom-call(bf16[1,1,48,128]{3,2,1,0:T(8,128)(2,1)} %x_ref.1, bf16[1,48,128]{2,1,0:T(8,128)(2,1)} %cot_ref.1, bf16[1,27,4608]{2,1,0:T(8,128)(2,1)} %w_ref.1, s32[27,1,128]{2,1,0:T(1,128)} %bitcast.3, s32[1,1,4,8]{3,2,1,0:T(4,128)} %list_ref.1), custom_call_target="tpu_custom_call" | custom-call | tf_op jit(solution)/shard_map/pallas_call | solution.py:402
  22.1 0.6 %copy.11 = bf16[1,1,48,128]{3,2,1,0:T(8,128)(2,1)} copy(bf16[1,1,48,128]{3,2,1,0:T(8,128)(2,1)S(1)} %get-tuple-element.12) | data formatting | bytes 24576
  22.7 0.8 %copy.12 = f32[1,27,4608]{2,0,1:T(1,128)} copy(f32[1,27,4608]{2,0,1:T(1,128)S(1)} %bitcast.2) | data formatting | bytes 995328
